TPU v7x, 32 devices: a whole 2x2x4 slice. The times are simulated.
32 devices in a mesh: freq: 8 (over y, x, core), blk: 4 (over z).
Axes of the slice: x: 2, y: 2, z: 4, core: 2. Of those that a mesh axis runs over, the one named last changes fastest.
Arguments:
- traces: bfloat16 [32, 4096, 1024], P(('blk', 'freq')), may hold values from -6 to 6
- fir: float32 [128], replicated, may hold values from -0.5 to 0.5
- targets: int32 [256], replicated, may hold values from 0 to 31
- band: int32 [2], replicated, may hold values from 1 to 512, as said below
Outputs:
- multiples: float32 [32, 2, 256, 4096], P('freq', None, None, 'blk')
Inputs may be any that keep to these rules, and one draw needn't show every extreme that they name: band[1] is 512 and band[1] - band[0] is at least 256.
All inputs are finite; a program needn't handle non-finite values.
Results may differ from a plain program's by a relative error of at most 0.019.
Values may be sent and summed in bfloat16 or wider, within the bound.
A program may use at most 128 MiB of HBM per device.

v0:
```python
import math
import jax
import jax.numpy as jnp
from jax import lax
from jax.sharding import PartitionSpec as P

FREQ_DEV = 4


def phase_table(band, freq_count, time_count):
    band_low = band[0]
    band_high = band[1]
    freq_index = jnp.arange(freq_count, dtype=jnp.int32)
    numerator = band_low * freq_count + (band_high - band_low) * freq_index
    time_index = jnp.arange(time_count, dtype=jnp.int32)
    turn_count = jnp.mod(time_index[:, None] * numerator[None, :], freq_count * time_count)
    phase_angle = turn_count.astype(jnp.float32) * (2.0 * math.pi / (freq_count * time_count))
    table = jnp.stack([jnp.cos(phase_angle), -jnp.sin(phase_angle)], axis=2) * (
        1.0 / math.sqrt(time_count)
    )
    return table.reshape(time_count, 2 * freq_count)


def split_parts(values):
    high_part = values.astype(jnp.bfloat16)
    low_part = (values - high_part.astype(jnp.float32)).astype(jnp.bfloat16)
    return (high_part, low_part)


def block_left(chosen):
    return jnp.stack(
        [
            jnp.concatenate([chosen[:, 0], -chosen[:, 1]], 1),
            jnp.concatenate([chosen[:, 1], chosen[:, 0]], 1),
        ],
        1,
    )


def column_products(chosen, columns, weight_scale):
    freq_dev, parts, shot_count, col_width = columns.shape
    right_block = columns.reshape(freq_dev, 2 * shot_count, col_width)
    summed = jnp.einsum(
        "fojk,fjr->fokr", block_left(chosen), right_block, preferred_element_type=jnp.float32
    )
    return summed * weight_scale


def local_targets(columns, targets, col_stride):
    picked = jnp.take(columns[..., ::col_stride], targets, axis=2)
    return jnp.swapaxes(picked, 2, 3)


def section_plan(spectrum, targets, col_stride, weight_scale):
    row_layout = lax.all_to_all(spectrum, "freq", split_axis=0, concat_axis=2, tiled=True)
    columns = lax.all_to_all(row_layout, "blk", split_axis=3, concat_axis=2, tiled=True)
    chosen = lax.all_gather(local_targets(columns, targets, col_stride), "blk", axis=2, tiled=True)
    return column_products(chosen, columns, weight_scale)


def per_device(traces, fir, targets, band):
    shot_dev, rec_count, time_count = traces.shape
    freq_devs = lax.axis_size("freq")
    blk_devs = lax.axis_size("blk")
    freq_count = FREQ_DEV * freq_devs
    shot_count = shot_dev * freq_devs * blk_devs
    col_stride = rec_count // shot_count
    tap_count = fir.shape[0]
    block_count = time_count // tap_count
    row_total = shot_dev * rec_count
    dft_table = phase_table(band, freq_count, time_count).reshape(
        block_count, tap_count, 2 * freq_count
    )
    tap_index = jnp.arange(tap_count, dtype=jnp.int32)
    lag_table = jnp.mod(tap_index[None, :] - tap_index[:, None], tap_count)
    circulant = jnp.sum(
        jnp.where(lag_table[:, :, None] == tap_index[None, None, :], fir[None, None, :], 0.0),
        axis=2,
    )
    lower_part = jnp.where(tap_index[None, :] >= tap_index[:, None], circulant, 0.0)
    upper_part = jnp.where(tap_index[None, :] < tap_index[:, None], circulant, 0.0)
    signal = traces.reshape(row_total, block_count, tap_count)
    lower_high, lower_low = split_parts(lower_part)
    upper_high, upper_low = split_parts(upper_part)
    earlier = signal[:, :-1]
    carried = jnp.einsum("rna,ab->rnb", earlier, upper_high, preferred_element_type=jnp.float32)
    carried = carried + jnp.einsum(
        "rna,ab->rnb", earlier, upper_low, preferred_element_type=jnp.float32
    )
    carried = jnp.concatenate([jnp.zeros((row_total, 1, tap_count), jnp.float32), carried], 1)
    shaped = jnp.einsum("rna,ab->rnb", signal, lower_high, preferred_element_type=jnp.float32)
    shaped = (
        shaped
        + jnp.einsum("rna,ab->rnb", signal, lower_low, preferred_element_type=jnp.float32)
        + carried
    )
    shaped_high, shaped_low = split_parts(shaped)
    table_high, table_low = split_parts(dft_table)
    spectrum = jnp.einsum(
        "rnb,nbc->cr", shaped_high, table_high, preferred_element_type=jnp.float32
    )
    spectrum = spectrum + jnp.einsum(
        "rnb,nbc->cr", shaped_high, table_low, preferred_element_type=jnp.float32
    )
    spectrum = spectrum + jnp.einsum(
        "rnb,nbc->cr", shaped_low, table_high, preferred_element_type=jnp.float32
    )
    spectrum = spectrum.astype(jnp.bfloat16).reshape(freq_count, 2, shot_dev, rec_count)
    weight_scale = 1.0 / math.sqrt(shot_count)
    return section_plan(spectrum, targets, col_stride, weight_scale)


def solution(mesh):
    placed = (P(("blk", "freq"), None, None), P(), P(), P())
    return jax.shard_map(
        per_device,
        mesh=mesh,
        in_specs=placed,
        out_specs=P("freq", None, None, "blk"),
        check_vma=False,
    )
```

profile of v0, /device:TPU:0, one launch (start us, length us, event | category | flops | bytes accessed | tf_op | source)
XLA Modules:
  0.0 191.2 jit_solution(4319317506778272300)
XLA Ops:
  0.0 11.9 %copy.90 = bf16[1,4096,1024]{1,2,0:T(8,128)(2,1)} copy(bf16[1,4096,1024]{2,1,0:T(8,128)(2,1)} %param.4) | data formatting | bytes 16777216 | tf_op args[0]
  12.0 5.1 %select_reduce_fusion = f32[128,128]{1,0:T(8,128)S(1)} fusion(f32[128]{0:T(128)S(1)} %copy-done.4, s32[128,128]{1,0:T(8,128)S(1)} %add_select_fusion.1), kind=kLoop, calls=%fused_computation.5 | loop fusion | flops 6275072 | bytes 131584 | tf_op jit(solution)/shard_map/reduce_sum | solution.py:76
  17.1 10.5 %fusion.1 = f32[128,4096,7]{1,0,2:T(8,128)} fusion(bf16[4096,8,128]{0,2,1:T(8,128)(2,1)} %bitcast.69, f32[128,128]{1,0:T(8,128)S(1)} %select_reduce_fusion), kind=kOutput, calls=%fused_computation.7 | convolution fusion | flops 939556864 | bytes 22085632 | tf_op jit(solution)/shard_map/rna,ab->rnb/dot_general | solution.py:86
  27.6 8.1 %fusion.29 = f32[128,4096,8]{1,0,2:T(8,128)} fusion(bf16[4096,8,128]{0,2,1:T(8,128)(2,1)S(1)} %bitcast.71, f32[128,128]{1,0:T(8,128)S(1)} %select_reduce_fusion), kind=kOutput, calls=%fused_computation.55 | convolution fusion | flops 1073774592 | bytes 25231360 | tf_op jit(solution)/shard_map/rna,ab->rnb/dot_general | solution.py:91
  35.7 9.4 %add_bitcast_fusion = f32[4096,7,128]{0,2,1:T(8,128)} fusion(f32[128,4096,7]{1,0,2:T(8,128)} %fusion.1, bf16[4096,8,128]{0,2,1:T(8,128)(2,1)S(1)} %bitcast.72, f32[128,128]{1,0:T(8,128)S(1)} %select_reduce_fusion), kind=kOutput, calls=%fused_computation.3 | convolution fusion | flops 943292416 | bytes 36765696 | tf_op jit(solution)/shard_map/rna,ab->rnb/dot_general | solution.py:87
  45.2 0.7 fusion.48
  47.8 0.6 fusion.20
  48.8 20.5 %bitcast_add_fusion = f32[4096,8,128]{0,2,1:T(8,128)} fusion(f32[4096,7,128]{0,2,1:T(8,128)} %add_bitcast_fusion, f32[128,4096,8]{1,0,2:T(8,128)} %fusion.29, bf16[4096,8,128]{0,2,1:T(8,128)(2,1)} %bitcast.70, f32[128,128]{1,0:T(8,128)S(1)} %select_reduce_fusion), kind=kOutput, calls=%fused_computation.1 | convolution fusion | flops 1082228736 | bytes 56688640 | tf_op jit(solution)/shard_map/rna,ab->rnb/dot_general | solution.py:94
  69.4 7.5 %convolution_bitcast_fusion.1 = f32[64,4096]{1,0:T(8,128)S(1)} fusion(f32[8,128,64]{1,0,2:T(8,128)S(1)} %mul.84, f32[4096,8,128]{0,2,1:T(8,128)} %bitcast_add_fusion), kind=kOutput, calls=%fused_computation.14 | convolution fusion | flops 541065216 | bytes 18087936 | tf_op jit(solution)/shard_map/rnb,nbc->cr/dot_general | solution.py:99
  76.9 3.1 %copy-done = f32[4096,8,128]{0,2,1:T(8,128)S(1)} copy-done((f32[4096,8,128]{0,2,1:T(8,128)S(1)}, f32[4096,8,128]{0,2,1:T(8,128)}, u32[]{:S(2)}) %copy-start) | copy-done | bytes 16777240
  79.9 1.6 fusion.4
  81.5 1.6 fusion.7
  83.4 14.7 %all_to_all.36 = bf16[32,2,1,4096]{3,1,2,0:T(2,128)(2,1)S(1)} all-to-all(bf16[32,2,1,4096]{3,1,2,0:T(2,128)(2,1)S(1)} %bitcast.78), channel_id=1, replica_groups=mesh['freq'=8,'blk'=4] {'freq'}, dimensions={0} | all-to-all | bytes 1048576 | tf_op jit(solution)/shard_map/all_to_all | solution.py:55
  98.1 9.2 %copy.103 = bf16[4,2,8,4096]{2,0,1,3:T(4,128)(2,1)} copy(bf16[4,2,8,4096]{3,1,0,2:T(2,128)(2,1)S(1)} %bitcast.77) | data formatting | bytes 1048576 | tf_op jit(solution)/shard_map/all_to_all | solution.py:55
  107.4 11.3 %reshape.170 = bf16[4,2,32768]{2,1,0:T(2,128)(2,1)} reshape(bf16[4096,2,4,8]{3,2,1,0:T(4,128)(2,1)} %bitcast.75) | data formatting | bytes 1048576
  118.7 4.8 %all-to-all-start.1 = ((bf16[4,2,32768]{2,1,0:T(2,128)(2,1)}), bf16[4,2,32768]{2,1,0:T(2,128)(2,1)S(1)}, u32[]{:S(2)}, u32[]{:S(2)}) async-start(bf16[4,2,32768]{2,1,0:T(2,128)(2,1)} %reshape.170), calls=%async_computation.1 | async-start | bytes 1048576 | tf_op jit(solution)/shard_map/all_to_all | solution.py:56
  123.6 13.8 %all-to-all-done.1 = bf16[4,2,32768]{2,1,0:T(2,128)(2,1)S(1)} async-done(((bf16[4,2,32768]{2,1,0:T(2,128)(2,1)}), bf16[4,2,32768]{2,1,0:T(2,128)(2,1)S(1)}, u32[]{:S(2)}, u32[]{:S(2)}) %all-to-all-start.1) | async-done | bytes 524320 | tf_op jit(solution)/shard_map/all_to_all | solution.py:56
  137.4 11.0 %reshape.171 = bf16[4096,2,4,8]{3,2,1,0:T(4,128)(2,1)} reshape(bf16[4,2,32768]{2,1,0:T(2,128)(2,1)S(1)} %all-to-all-done.1) | data formatting | bytes 1048576
  148.4 11.7 %copy.105 = bf16[4,2,4,8,1024]{4,0,3,2,1:T(4,128)(2,1)S(1)} copy(bf16[4,2,4,8,1024]{3,0,1,4,2:T(4,128)(2,1)} %bitcast.73) | data formatting | bytes 1048576 | tf_op jit(solution)/shard_map/all_to_all | solution.py:56
  160.1 0.7 slice.23
  160.8 1.2 gather_fusion
  162.3 13.3 %all_gather.3 = bf16[4,2,32,256]{3,2,0,1:T(8,128)(2,1)S(1)} all-gather(bf16[4,2,8,256]{3,2,0,1:T(8,128)(2,1)S(1)} %select_bitcast_fusion), channel_id=1, replica_groups=mesh['freq'=8,'blk'=4] {'blk'}, dimensions={2}, use_global_device_ids=true | all-gather | bytes 163840 | tf_op jit(solution)/shard_map/all_gather | solution.py:57
  175.7 10.8 %copy.108 = bf16[4,2,4,8,1024]{4,3,2,1,0:T(8,128)(2,1)S(1)} copy(bf16[4,2,4,8,1024]{3,0,1,4,2:T(4,128)(2,1)} %bitcast.74) | data formatting | bytes 1048576 | tf_op jit(solution)/shard_map/all_to_all | solution.py:56
  186.5 4.7 %broadcast_multiply_fusion = f32[4,2,256,1024]{3,2,1,0:T(8,128)} fusion(bf16[4,64,1024,1]{2,1,3,0:T(8,128)(2,1)S(1)} %bitcast.76, bf16[4,1,64,256]{3,2,1,0:T(8,128)(2,1)S(1)} %get-tuple-element.8, bf16[4,1,64,256]{3,2,1,0:T(8,128)(2,1)S(1)} %get-tuple-element.7), kind=kOutput, calls=%fused_computation.16 | convolution fusion | flops 270663680 | bytes 9175040 | tf_op jit(solution)/shard_map/fojk,fjr->fokr/dot_general | solution.py:43
  (23 shorter events, 1.2 us)
Async XLA Ops:
  0.0 11.9 %copy-start.4 = (f32[128]{0:T(128)S(1)}, f32[128]{0:T(128)}, u32[]{:S(2)}) copy-start(f32[128]{0:T(128)} %param.5) | copy-start | bytes 1540
  17.1 10.5 %copy-start.1 = (bf16[1,4096,1024]{1,2,0:T(8,128)(2,1)S(1)}, bf16[1,4096,1024]{1,2,0:T(8,128)(2,1)}, u32[]{:S(2)}) copy-start(bf16[1,4096,1024]{1,2,0:T(8,128)(2,1)} %copy.90) | copy-start | bytes 25165828
  35.7 9.5 %copy-start.2 = (s32[2]{0:T(128)S(1)}, s32[2]{0:T(128)}, u32[]{:S(2)}) copy-start(s32[2]{0:T(128)} %param.7) | copy-start | bytes 28
  69.4 10.5 %copy-start = (f32[4096,8,128]{0,2,1:T(8,128)S(1)}, f32[4096,8,128]{0,2,1:T(8,128)}, u32[]{:S(2)}) copy-start(f32[4096,8,128]{0,2,1:T(8,128)} %bitcast_add_fusion) | copy-start | bytes 50331652
  98.1 25.4 %copy-start.3 = (s32[256]{0:T(256)S(1)}, s32[256]{0:T(256)}, u32[]{:S(2)}) copy-start(s32[256]{0:T(256)} %param.6) | copy-start | bytes 3076
  118.7 18.7 %all-to-all-start.1 = ((bf16[4,2,32768]{2,1,0:T(2,128)(2,1)}), bf16[4,2,32768]{2,1,0:T(2,128)(2,1)S(1)}, u32[]{:S(2)}, u32[]{:S(2)}) async-start(bf16[4,2,32768]{2,1,0:T(2,128)(2,1)} %reshape.170), calls=%async_computation.1 | async-start | bytes 1048576 | tf_op jit(solution)/shard_map/all_to_all | solution.py:56
where the time goes:
time: 192 us; the launch traced here: 191 us
  local copies, waits for them, and re-layouts  72.7 us (38%)
  matrix products  63.9 us (33%)
  blocking collectives  28.1 us (15%)
  waiting for transfers between devices  13.8 us (7%)
  other arithmetic  5.83 us (3%)
  starting transfers between devices  4.85 us (3%)
  between operations  2.08 us (1%)
    unnamed x13, local copies, waits for them, and re-layouts  37.3 us
    all_to_all x2, local copies, waits for them, and re-layouts, section_plan(): lax.all_to_all(row_layout, 'blk', split_axis=3, concat_axis=2, tiled=True)  22.5 us
    dot_general x1, matrix products, per_device(): jnp.einsum('rna,ab->rnb', signal, lower_low, preferred_element_type=jnp.f...  20.5 us
    all_to_all x1, blocking collectives, section_plan(): lax.all_to_all(spectrum, 'freq', split_axis=0, concat_axis=2, tiled=True)  14.7 us
    all_to_all x1, waiting for transfers between devices, section_plan(): lax.all_to_all(row_layout, 'blk', split_axis=3, concat_axis=2, tiled=True)  13.8 us
    all_gather x1, blocking collectives, section_plan(): lax.all_gather(local_targets(columns, targets, col_stride), 'blk', axis=2...  13.3 us
    dot_general x1, matrix products, per_device(): jnp.einsum('rna,ab->rnb', earlier, upper_high, preferred_element_type=jnp...  10.5 us
    dot_general x1, matrix products, per_device(): jnp.einsum('rna,ab->rnb', earlier, upper_low, preferred_element_type=jnp....  9.45 us
  transfers between devices with their start and end apart: 1, of which 1 were waited for; matrix products, arithmetic and copies ran while one was open for 0% of the time, Pallas kernels for 0%

commit v1 on v0

--- a/solution.py
+++ b/solution.py
@@ -5,6 +5,23 @@
 from jax.sharding import PartitionSpec as P
 
 FREQ_DEV = 4
+
+
+def lead_outputs(xx):
+    link_axis = "blk"
+    front = jax.lax.axis_size(link_axis)
+    raw_out, block_last, z_new = (front, jax.lax.axis_index(link_axis), xx.shape[2])
+    kept_arr, b_next = (xx, 1)
+    while b_next < raw_out:
+        grid = []
+        dev = 0
+        while dev < raw_out:
+            grid.append((dev, (dev - b_next) % raw_out))
+            dev += 1
+        piece_now = jax.lax.ppermute(kept_arr, link_axis, grid)
+        kept_arr = jnp.concatenate([kept_arr, piece_now], axis=2)
+        b_next = 2 * b_next
+    return jnp.roll(kept_arr, block_last * z_new, axis=2)
 
 
 def phase_table(band, freq_count, time_count):
@@ -54,7 +71,7 @@
 def section_plan(spectrum, targets, col_stride, weight_scale):
     row_layout = lax.all_to_all(spectrum, "freq", split_axis=0, concat_axis=2, tiled=True)
     columns = lax.all_to_all(row_layout, "blk", split_axis=3, concat_axis=2, tiled=True)
-    chosen = lax.all_gather(local_targets(columns, targets, col_stride), "blk", axis=2, tiled=True)
+    chosen = lead_outputs(local_targets(columns, targets, col_stride))
     return column_products(chosen, columns, weight_scale)
 
 

time: 192 us -> 186 us (0.969)
  blocking collectives: 28.1 us -> 14.7 us
  waiting for transfers between devices: 13.8 us -> 19.6 us
    all_gather x1 -> x0, blocking collectives: 13.3 us -> none  [section_plan(): lax.all_gather(local_targets(columns, targets, col_stride), 'blk', axis=2...]
    ppermute x0 -> x2, waiting for transfers between devices: none -> 5.84 us  [lead_outputs(): piece_now = jax.lax.ppermute(kept_arr, link_axis, grid)]
    unnamed x13 -> x17, local copies, waits for them, and re-layouts: 37.3 us -> 37.3 us
  transfers between devices with their start and end apart: 1 -> 3, of which waited for: 1 -> 2; matrix products, arithmetic and copies ran while one was open for 0% -> 6% of each run, Pallas kernels for 0% -> 0%
where the time goes in v1:
time: 186 us; the launch traced here: 185 us
  local copies, waits for them, and re-layouts  72.7 us (39%)
  matrix products  63.9 us (34%)
  waiting for transfers between devices  19.6 us (11%)
  blocking collectives  14.7 us (8%)
  starting transfers between devices  6.46 us (3%)
  other arithmetic  5.85 us (3%)
  between operations  2.3 us (1%)
    unnamed x17, local copies, waits for them, and re-layouts  37.3 us
    all_to_all x2, local copies, waits for them, and re-layouts, section_plan(): lax.all_to_all(row_layout, 'blk', split_axis=3, concat_axis=2, tiled=True)  22.5 us
    dot_general x1, matrix products, per_device(): jnp.einsum('rna,ab->rnb', signal, lower_low, preferred_element_type=jnp.f...  20.5 us
    all_to_all x1, blocking collectives, section_plan(): lax.all_to_all(spectrum, 'freq', split_axis=0, concat_axis=2, tiled=True)  14.7 us
    all_to_all x1, waiting for transfers between devices, section_plan(): lax.all_to_all(row_layout, 'blk', split_axis=3, concat_axis=2, tiled=True)  13.8 us
    dot_general x1, matrix products, per_device(): jnp.einsum('rna,ab->rnb', earlier, upper_high, preferred_element_type=jnp...  10.5 us
    dot_general x1, matrix products, per_device(): jnp.einsum('rna,ab->rnb', earlier, upper_low, preferred_element_type=jnp....  9.39 us
    all_to_all x1, local copies, waits for them, and re-layouts, section_plan(): lax.all_to_all(spectrum, 'freq', split_axis=0, concat_axis=2, tiled=True)  9.24 us
  transfers between devices with their start and end apart: 3, of which 2 were waited for; matrix products, arithmetic and copies ran while one was open for 6% of the time, Pallas kernels for 0%

profile of v1, /device:TPU:0, one launch (start us, length us, event | category | flops | bytes accessed | tf_op | source)
XLA Modules:
  0.0 185.5 jit_solution(14612912469226271875)
XLA Ops:
  0.0 11.9 %copy.90 = bf16[1,4096,1024]{1,2,0:T(8,128)(2,1)} copy(bf16[1,4096,1024]{2,1,0:T(8,128)(2,1)} %param.4) | data formatting | bytes 16777216 | tf_op args[0]
  12.0 5.1 %select_reduce_fusion = f32[128,128]{1,0:T(8,128)S(1)} fusion(f32[128]{0:T(128)S(1)} %copy-done.4, s32[128,128]{1,0:T(8,128)S(1)} %add_select_fusion.1), kind=kLoop, calls=%fused_computation.5 | loop fusion | flops 6275072 | bytes 131584 | tf_op jit(solution)/shard_map/reduce_sum | solution.py:93
  17.1 10.5 %fusion.1 = f32[128,4096,7]{1,0,2:T(8,128)} fusion(bf16[4096,8,128]{0,2,1:T(8,128)(2,1)} %bitcast.69, f32[128,128]{1,0:T(8,128)S(1)} %select_reduce_fusion), kind=kOutput, calls=%fused_computation.7 | convolution fusion | flops 939556864 | bytes 22085632 | tf_op jit(solution)/shard_map/rna,ab->rnb/dot_general | solution.py:103
  27.6 8.1 %fusion.29 = f32[128,4096,8]{1,0,2:T(8,128)} fusion(bf16[4096,8,128]{0,2,1:T(8,128)(2,1)S(1)} %bitcast.71, f32[128,128]{1,0:T(8,128)S(1)} %select_reduce_fusion), kind=kOutput, calls=%fused_computation.56 | convolution fusion | flops 1073774592 | bytes 25231360 | tf_op jit(solution)/shard_map/rna,ab->rnb/dot_general | solution.py:108
  35.8 9.4 %add_bitcast_fusion = f32[4096,7,128]{0,2,1:T(8,128)} fusion(f32[128,4096,7]{1,0,2:T(8,128)} %fusion.1, bf16[4096,8,128]{0,2,1:T(8,128)(2,1)S(1)} %bitcast.72, f32[128,128]{1,0:T(8,128)S(1)} %select_reduce_fusion), kind=kOutput, calls=%fused_computation.3 | convolution fusion | flops 943292416 | bytes 36765696 | tf_op jit(solution)/shard_map/rna,ab->rnb/dot_general | solution.py:104
  45.2 0.7 fusion.48
  49.0 20.5 %bitcast_add_fusion = f32[4096,8,128]{0,2,1:T(8,128)} fusion(f32[4096,7,128]{0,2,1:T(8,128)} %add_bitcast_fusion, f32[128,4096,8]{1,0,2:T(8,128)} %fusion.29, bf16[4096,8,128]{0,2,1:T(8,128)(2,1)} %bitcast.70, f32[128,128]{1,0:T(8,128)S(1)} %select_reduce_fusion), kind=kOutput, calls=%fused_computation.1 | convolution fusion | flops 1082228736 | bytes 56688640 | tf_op jit(solution)/shard_map/rna,ab->rnb/dot_general | solution.py:111
  69.5 7.5 %convolution_bitcast_fusion.1 = f32[64,4096]{1,0:T(8,128)S(1)} fusion(f32[8,128,64]{1,0,2:T(8,128)S(1)} %mul.87, f32[4096,8,128]{0,2,1:T(8,128)} %bitcast_add_fusion), kind=kOutput, calls=%fused_computation.14 | convolution fusion | flops 541065216 | bytes 18087936 | tf_op jit(solution)/shard_map/rnb,nbc->cr/dot_general | solution.py:116
  77.0 3.1 %copy-done = f32[4096,8,128]{0,2,1:T(8,128)S(1)} copy-done((f32[4096,8,128]{0,2,1:T(8,128)S(1)}, f32[4096,8,128]{0,2,1:T(8,128)}, u32[]{:S(2)}) %copy-start) | copy-done | bytes 16777240
  80.0 1.6 fusion.4
  81.6 1.6 fusion.7
  83.5 14.7 %all_to_all.36 = bf16[32,2,1,4096]{3,1,2,0:T(2,128)(2,1)S(1)} all-to-all(bf16[32,2,1,4096]{3,1,2,0:T(2,128)(2,1)S(1)} %bitcast.78), channel_id=1, replica_groups=mesh['freq'=8,'blk'=4] {'freq'}, dimensions={0} | all-to-all | bytes 1048576 | tf_op jit(solution)/shard_map/all_to_all | solution.py:72
  98.2 9.2 %copy.103 = bf16[4,2,8,4096]{2,0,1,3:T(4,128)(2,1)} copy(bf16[4,2,8,4096]{3,1,0,2:T(2,128)(2,1)S(1)} %bitcast.77) | data formatting | bytes 1048576 | tf_op jit(solution)/shard_map/all_to_all | solution.py:72
  107.5 11.3 %reshape.170 = bf16[4,2,32768]{2,1,0:T(2,128)(2,1)} reshape(bf16[4096,2,4,8]{3,2,1,0:T(4,128)(2,1)} %bitcast.75) | data formatting | bytes 1048576
  118.8 4.9 %all-to-all-start.1 = ((bf16[4,2,32768]{2,1,0:T(2,128)(2,1)}), bf16[4,2,32768]{2,1,0:T(2,128)(2,1)S(1)}, u32[]{:S(2)}, u32[]{:S(2)}) async-start(bf16[4,2,32768]{2,1,0:T(2,128)(2,1)} %reshape.170), calls=%async_computation.1 | async-start | bytes 1048576 | tf_op jit(solution)/shard_map/all_to_all | solution.py:73
  123.7 13.8 %all-to-all-done.1 = bf16[4,2,32768]{2,1,0:T(2,128)(2,1)S(1)} async-done(((bf16[4,2,32768]{2,1,0:T(2,128)(2,1)}), bf16[4,2,32768]{2,1,0:T(2,128)(2,1)S(1)}, u32[]{:S(2)}, u32[]{:S(2)}) %all-to-all-start.1) | async-done | bytes 524320 | tf_op jit(solution)/shard_map/all_to_all | solution.py:73
  137.5 11.0 %reshape.171 = bf16[4096,2,4,8]{3,2,1,0:T(4,128)(2,1)} reshape(bf16[4,2,32768]{2,1,0:T(2,128)(2,1)S(1)} %all-to-all-done.1) | data formatting | bytes 1048576
  148.5 11.7 %copy.105 = bf16[4,2,4,8,1024]{4,0,3,2,1:T(4,128)(2,1)S(1)} copy(bf16[4,2,4,8,1024]{3,0,1,4,2:T(4,128)(2,1)} %bitcast.73) | data formatting | bytes 1048576 | tf_op jit(solution)/shard_map/all_to_all | solution.py:73
  160.2 0.7 slice.23
  160.9 1.2 gather_fusion
  162.5 1.5 collective-permute-start
  164.0 10.7 %copy.108 = bf16[4,2,4,8,1024]{4,3,2,1,0:T(8,128)(2,1)S(1)} copy(bf16[4,2,4,8,1024]{3,0,1,4,2:T(4,128)(2,1)} %bitcast.74) | data formatting | bytes 1048576 | tf_op jit(solution)/shard_map/all_to_all | solution.py:73
  174.8 5.8 %collective-permute-done.1 = bf16[4,2,16,256]{3,2,0,1:T(8,128)(2,1)S(1)} collective-permute-done((bf16[4,2,16,256]{3,2,0,1:T(8,128)(2,1)S(1)}, bf16[4,2,16,256]{3,2,0,1:T(8,128)(2,1)S(1)}, u32[]{:S(2)}, u32[]{:S(2)}) %collective-permute-start.1) | collective-permute-done | bytes 65568 | tf_op jit(solution)/shard_map/ppermute | solution.py:21
  180.8 4.7 %broadcast_multiply_fusion = f32[4,2,256,1024]{3,2,1,0:T(8,128)} fusion(bf16[4,64,1024,1]{2,1,3,0:T(8,128)(2,1)S(1)} %bitcast.76, bf16[4,1,64,256]{3,2,1,0:T(8,128)(2,1)S(1)} %get-tuple-element.10, bf16[4,1,64,256]{3,2,1,0:T(8,128)(2,1)S(1)} %get-tuple-element.9), kind=kOutput, calls=%fused_computation.16 | convolution fusion | flops 270663680 | bytes 9175040 | tf_op jit(solution)/shard_map/fojk,fjr->fokr/dot_general | solution.py:60
  (32 shorter events, 1.9 us)
Async XLA Ops:
  0.0 11.9 %copy-start.4 = (f32[128]{0:T(128)S(1)}, f32[128]{0:T(128)}, u32[]{:S(2)}) copy-start(f32[128]{0:T(128)} %param.5) | copy-start | bytes 1540
  17.1 10.5 %copy-start.1 = (bf16[1,4096,1024]{1,2,0:T(8,128)(2,1)S(1)}, bf16[1,4096,1024]{1,2,0:T(8,128)(2,1)}, u32[]{:S(2)}) copy-start(bf16[1,4096,1024]{1,2,0:T(8,128)(2,1)} %copy.90) | copy-start | bytes 25165828
  35.8 9.4 %copy-start.2 = (s32[2]{0:T(128)S(1)}, s32[2]{0:T(128)}, u32[]{:S(2)}) copy-start(s32[2]{0:T(128)} %param.7) | copy-start | bytes 28
  69.5 10.5 %copy-start = (f32[4096,8,128]{0,2,1:T(8,128)S(1)}, f32[4096,8,128]{0,2,1:T(8,128)}, u32[]{:S(2)}) copy-start(f32[4096,8,128]{0,2,1:T(8,128)} %bitcast_add_fusion) | copy-start | bytes 50331652
  98.2 25.4 %copy-start.3 = (s32[256]{0:T(256)S(1)}, s32[256]{0:T(256)}, u32[]{:S(2)}) copy-start(s32[256]{0:T(256)} %param.6) | copy-start | bytes 3076
  118.8 18.7 %all-to-all-start.1 = ((bf16[4,2,32768]{2,1,0:T(2,128)(2,1)}), bf16[4,2,32768]{2,1,0:T(2,128)(2,1)S(1)}, u32[]{:S(2)}, u32[]{:S(2)}) async-start(bf16[4,2,32768]{2,1,0:T(2,128)(2,1)} %reshape.170), calls=%async_computation.1 | async-start | bytes 1048576 | tf_op jit(solution)/shard_map/all_to_all | solution.py:73
  162.5 12.3 %collective-permute-start = (bf16[4,2,8,256]{3,2,0,1:T(8,128)(2,1)S(1)}, bf16[4,2,8,256]{3,2,0,1:T(8,128)(2,1)S(1)}, u32[]{:S(2)}, u32[]{:S(2)}) collective-permute-start(bf16[4,2,8,256]{3,2,0,1:T(8,128)(2,1)S(1)} %get-tuple-element.8), channel_id=1, source_target_pairs={{0,3},{1,0},{2,1},{3,2},{4,7},{5,4},{6,5},{7,6},{8,11},{9,8},{10,9... | collective-permute-start | bytes 98312 | tf_op jit(solution)/shard_map/ppermute | solution.py:21
  174.7 5.9 %collective-permute-start.1 = (bf16[4,2,16,256]{3,2,0,1:T(8,128)(2,1)S(1)}, bf16[4,2,16,256]{3,2,0,1:T(8,128)(2,1)S(1)}, u32[]{:S(2)}, u32[]{:S(2)}) collective-permute-start(bf16[4,2,16,256]{3,2,0,1:T(8,128)(2,1)S(1)} %pad_maximum_fusion), channel_id=1, source_target_pairs={{0,2},{1,3},{2,0},{3,1},{4,6},{5,7},{6,4},{7,5},{8,10},{9,11},{10,... | collective-permute-start | bytes 196616 | tf_op jit(solution)/shard_map/ppermute | solution.py:21
